TPU v7x, 32 devices: a whole 2x2x4 slice. The times are simulated.
32 devices in a mesh: ctx: 8 (over z, y), head: 4 (over x, core).
Axes of the slice: x: 2, y: 2, z: 4, core: 2. Of those that a mesh axis runs over, the one named last changes fastest.
Arguments:
- queries: bfloat16 [8192, 4096], P('ctx', 'head'), as said below
- key_value: bfloat16 [2, 8192, 4096], P(None, 'ctx', 'head'), as said below
- lanczos_vec: float32 [8192, 4096], P('ctx', 'head'), as said below
- rand_blocks: int32 [64, 3], replicated, may hold values from 0 to 63, as said below
- global_ids: int32 [2], replicated, may hold values from 0 to 63
Outputs:
- next_vec: float32 [8192, 4096], P('ctx', 'head')
- coefficients: float32 [2], replicated
Inputs may be any that keep to these rules, and one draw needn't show every extreme that they name: `rand_blocks`: row b lists the random key blocks of query block b. For each shard of 8 query blocks along ctx and each shard of 8 key blocks, at most 3 of the shard's listed random blocks lie in that key shard, and every query shard reaches 3 with some key shard. `queries`: entries are of order one or a few tens. `key_value`: keys of order one, values of order one to a few hundred. `lanczos_vec`: nonzero real entries; the mean of their squares over all entries is one, up to float32 rounding.
All inputs are finite; a program needn't handle non-finite values.
Results may differ from a plain program's by a relative error of at most 0.0049.
Values may be sent and summed in bfloat16 or wider, within the bound.
A program may use at most 192 MiB of HBM per device.

v0:
```python
import jax
import jax.numpy as jnp
from jax import lax
from jax.sharding import PartitionSpec as P

HD = 128
BS = 128


def padded_2(cells, sides, width):
    for axis, dim in sides:
        count = lax.axis_size(axis)
        ends = count - 1
        head = lax.slice_in_dim(cells, 0, width, axis=dim)
        tail = lax.slice_in_dim(cells, cells.shape[dim] - width, cells.shape[dim], axis=dim)
        cells = jnp.concatenate(
            [
                lax.ppermute(tail, axis, [(i, (i + 1) % count) for i in range(ends)]),
                cells,
                lax.ppermute(head, axis, [((i + 1) % count, i) for i in range(ends)]),
            ],
            axis=dim,
        )
    return cells


def from_root(block, axis, holder):
    block = jnp.where(lax.axis_index(axis) == holder, block, jnp.zeros_like(block))
    return lax.psum(block, axis)


def local(queries, key_value, lanczos_vec, rand_blocks, global_ids):
    tok_rows = queries.shape[0]
    col_width = queries.shape[1]
    nblocks = tok_rows // BS
    local_heads = col_width // HD
    ctx_count = lax.axis_size("ctx")
    ctx_index = lax.axis_index("ctx")
    random_count = rand_blocks.shape[1]
    glob_count = global_ids.shape[0]
    capacity = (nblocks * random_count + ctx_count - 1) // ctx_count
    score_scale = HD ** (-0.5)
    blocks_kv = key_value.reshape(2, nblocks, BS, col_width)
    padded = padded_2(key_value, (("ctx", 1),), BS)
    window = jnp.concatenate(
        [
            padded[:, offset * BS : offset * BS + tok_rows].reshape(2, nblocks, BS, col_width)
            for offset in range(3)
        ],
        axis=2,
    )
    owners = global_ids // nblocks
    places = global_ids % nblocks
    requests = rand_blocks.reshape(ctx_count, nblocks * random_count)
    sources = requests // nblocks
    inside = requests % nblocks
    is_mine = (sources == ctx_index).astype(jnp.int32)
    earlier = jnp.cumsum(is_mine, axis=1) - is_mine
    slot_ids = jnp.arange(capacity, dtype=jnp.int32)
    matched = (is_mine[:, :, None] == 1) & (earlier[:, :, None] == slot_ids[None, None, :])
    chosen = jnp.sum(jnp.where(matched, inside[:, :, None], 0), axis=1)
    outgoing = jnp.take(blocks_kv, chosen.reshape(-1), axis=1)
    own_list = lax.dynamic_index_in_dim(requests, ctx_index, 0, keepdims=False)
    own_sources = own_list // nblocks
    request_total = own_list.shape[0]
    before_mask = jnp.arange(request_total)[:, None] > jnp.arange(request_total)[None, :]
    same_source = own_sources[:, None] == own_sources[None, :]
    order_rank = jnp.sum((before_mask & same_source).astype(jnp.int32), axis=1)
    pieces = []
    for global_pos in range(glob_count):
        block_piece = lax.dynamic_slice_in_dim(key_value, places[global_pos] * BS, BS, 1)
        pieces.append(from_root(block_piece, "ctx", owners[global_pos]))
    global_kv = jnp.concatenate(pieces, axis=1)
    incoming = lax.all_to_all(outgoing, "ctx", split_axis=1, concat_axis=1, tiled=True)
    random_kv = jnp.take(incoming, own_sources * capacity + order_rank, axis=1)
    random_kv = random_kv.reshape(2, nblocks, random_count * BS, col_width)
    global_wide = jnp.broadcast_to(global_kv[:, None], (2, nblocks, glob_count * BS, col_width))
    listed_kv = jnp.concatenate([window, global_wide, random_kv], axis=2)
    key_total = listed_kv.shape[2]
    key_position = jnp.arange(key_total)[None, :]
    block_index = jnp.arange(nblocks)[:, None]
    left_bad = (block_index == 0) & (key_position < BS) & (ctx_index == 0)
    right_bad = (
        (block_index == nblocks - 1)
        & (key_position >= 2 * BS)
        & (key_position < 3 * BS)
        & (ctx_index == ctx_count - 1)
    )
    valid_keys = jnp.logical_not(left_bad | right_bad)
    group_size = min(nblocks, max(1, 512 // BS))
    group_count = nblocks // group_size
    query_groups = queries.reshape(group_count, group_size, BS, local_heads, HD)
    tangent_groups = lanczos_vec.astype(jnp.bfloat16).reshape(
        group_count, group_size, BS, local_heads, HD
    )
    key_groups = listed_kv[0].reshape(group_count, group_size, key_total, local_heads, HD)
    value_groups = listed_kv[1].reshape(group_count, group_size, key_total, local_heads, HD)
    valid_groups = valid_keys.reshape(group_count, group_size, key_total)

    def attend(inputs_group):
        query_part, tangent, key_part, values, valid_part = inputs_group
        valid_wide = valid_part[:, None, None, :]
        scores = (
            jnp.einsum("bqhd,bkhd->bhqk", query_part, key_part, preferred_element_type=jnp.float32)
            * score_scale
        )
        row_top = jnp.max(jnp.where(valid_wide, scores, -jnp.inf), axis=-1, keepdims=True)
        weights = jnp.where(valid_wide, jnp.exp(scores - row_top), 0.0)
        attention = weights / jnp.sum(weights, axis=-1, keepdims=True)
        dscore = (
            jnp.einsum("bqhd,bkhd->bhqk", tangent, key_part, preferred_element_type=jnp.float32)
            * score_scale
        )
        center = jnp.sum(attention * dscore, axis=-1, keepdims=True)
        first_grad = (attention * (dscore - center)).astype(jnp.bfloat16)
        tangent_out = jnp.einsum(
            "bhqk,bkhd->bqhd", first_grad, values, preferred_element_type=jnp.float32
        ).astype(jnp.bfloat16)
        back_prob = jnp.einsum(
            "bqhd,bkhd->bhqk", tangent_out, values, preferred_element_type=jnp.float32
        )
        center_two = jnp.sum(attention * back_prob, axis=-1, keepdims=True)
        second_grad = (attention * (back_prob - center_two)).astype(jnp.bfloat16)
        return (
            jnp.einsum("bhqk,bkhd->bqhd", second_grad, key_part, preferred_element_type=jnp.float32)
            * score_scale
        )

    product = lax.map(
        attend, (query_groups, tangent_groups, key_groups, value_groups, valid_groups)
    )
    product = product.reshape(tok_rows, col_width)
    entry_count = float(tok_rows * col_width * ctx_count * lax.axis_size("head"))
    cross_sum, image_sum, vector_sum = lax.psum(
        (
            jnp.sum(lanczos_vec * product),
            jnp.sum(product * product),
            jnp.sum(lanczos_vec * lanczos_vec),
        ),
        ("ctx", "head"),
    )
    alpha_coef = cross_sum / entry_count
    residual = product - alpha_coef * lanczos_vec
    square_sum = image_sum - 2.0 * alpha_coef * cross_sum + alpha_coef * alpha_coef * vector_sum
    beta_coef = jnp.sqrt(square_sum / entry_count + 1e-06)
    coefficients = jnp.stack([alpha_coef, beta_coef])
    return (residual / beta_coef, coefficients)


def solution(mesh):
    placed = (P("ctx", "head"), P(None, "ctx", "head"), P("ctx", "head"), P(), P())
    return jax.shard_map(
        local, mesh=mesh, in_specs=placed, out_specs=(P("ctx", "head"), P()), check_vma=False
    )
```

profile of v0, /device:TPU:0, one launch (start us, length us, event | category | flops | bytes accessed | tf_op | source)
XLA Modules:
  0.0 716.1 jit_solution(8905988775322343834)
XLA Ops:
  8.7 8.2 %gather_fusion = bf16[24,2,128,1024]{3,2,1,0:T(8,128)(2,1)} fusion(bf16[2,8,128,1024]{3,2,1,0:T(8,128)(2,1)} %bitcast.135, s32[1024]{0:T(1024)S(1)} %pad_clamp_fusion.1), kind=kCustom, calls=%fused_computation | custom fusion | bytes 25165920 | tf_op jit(solution)/shard_map/jit(_take)/gather | solution.py:62
  16.9 10.7 %select_bitcast_fusion = bf16[2,24,128,1024]{3,2,0,1:T(8,128)(2,1)} fusion(bf16[24,2,128,1024]{3,2,1,0:T(8,128)(2,1)} %gather_fusion, pred[24]{0:T(512)(128)(4,1)S(1)} %compare_and_fusion), kind=kLoop, calls=%fused_computation.50 | loop fusion | flops 6291456 | bytes 25165848 | tf_op jit(solution)/shard_map/jit(_take)/select_n | solution.py:62
  27.6 7.3 %all-to-all-start = ((bf16[2,24,128,1024]{3,2,0,1:T(8,128)(2,1)}), bf16[2,24,128,1024]{3,2,0,1:T(8,128)(2,1)}, u32[]{:S(2)}, u32[]{:S(2)}) async-start(bf16[2,24,128,1024]{3,2,0,1:T(8,128)(2,1)} %select_bitcast_fusion), calls=%async_computation | async-start | bytes 25165824 | tf_op jit(solution)/shard_map/all_to_all | solution.py:74
  59.1 94.2 %collective-permute-done = bf16[2,128,1024]{2,1,0:T(8,128)(2,1)} collective-permute-done((bf16[2,128,1024]{2,1,0:T(8,128)(2,1)S(1)}, bf16[2,128,1024]{2,1,0:T(8,128)(2,1)}, u32[]{:S(2)}, u32[]{:S(2)}) %collective-permute-start) | collective-permute-done | bytes 524320 | tf_op jit(solution)/shard_map/ppermute | solution.py:18
  164.3 198.7 %all-reduce.4.cloned.1.call-done = (bf16[2,128,1024]{2,1,0:T(8,128)(2,1)}, bf16[2,128,1024]{2,1,0:T(8,128)(2,1)}) async-done(((bf16[2,128,1024]{2,1,0:T(8,128)(2,1)}, bf16[2,128,1024]{2,1,0:T(8,128)(2,1)}), (bf16[2,128,1024]{2,1,0:T(8,128)(2,1)}, bf16[2,128,1024]{2,1,0:T(8,128)(2,1)})) %all-reduce.4.cloned.1.call-update) | async-done | bytes 1048592 | tf_op jit(solution)/shard_map/psum | solution.py:29
  368.5 10.6 %gather_fusion.1 = bf16[24,2,128,1024]{3,2,1,0:T(8,128)(2,1)} fusion(bf16[2,24,128,1024]{3,2,0,1:T(8,128)(2,1)} %all-to-all-done, s32[1024]{0:T(1024)S(1)} %pad_clamp_fusion), kind=kCustom, calls=%fused_computation.1 | custom fusion | bytes 25165920 | tf_op jit(solution)/shard_map/jit(_take)/gather | solution.py:75
  379.1 6.5 copy.46
  385.5 5.8 fusion.45
  391.3 23.0 %fusion.68 = (bf16[1,8,1024,1024]{3,2,1,0:T(8,128)(2,1)}, bf16[1,8,1024,1024]{3,2,1,0:T(8,128)(2,1)}) fusion(bf16[2,8,1024,1024]{3,2,1,0:T(8,128)(2,1)} %fusion.45), kind=kLoop, calls=%fused_computation.136 | loop fusion | bytes 67108864 | tf_op jit(solution)/shard_map/slice | solution.py:97
  414.4 21.6 %copy.47 = bf16[1,8,1024,1024]{2,3,1,0:T(8,128)(2,1)} copy(bf16[1,8,1024,1024]{3,2,1,0:T(8,128)(2,1)} %get-tuple-element.95) | data formatting | bytes 33554432 | tf_op jit(solution)/shard_map/slice | solution.py:96
  435.9 21.6 %copy.48 = bf16[1,8,1024,1024]{2,3,1,0:T(8,128)(2,1)} copy(bf16[1,8,1024,1024]{3,2,1,0:T(8,128)(2,1)} %get-tuple-element.94) | data formatting | bytes 33554432 | tf_op jit(solution)/shard_map/slice | solution.py:97
  457.5 185.1 %while.10 = (s32[]{:T(128)}, f32[2,4,128,8,128]{2,4,3,1,0:T(8,128)}, bf16[2,4,1024,8,128]{2,4,3,1,0:T(8,128)(2,1)}, pred[2,4,1024]{2,1,0:T(4,128)(4,1)S(1)}, bf1...) while((s32[]{:T(128)}, ...), condition=%wide.region_10.11_spmd, body=%wide.region_5.10_spmd.sunk | while | flops 5462025216 | bytes 235043936 | solution.py:129
  458.8 11.4 %fusion.79 = f32[4,8,128,1024]{3,2,1,0:T(8,128)} fusion(bf16[2,4,1024,8,128]{2,4,3,1,0:T(8,128)(2,1)} %get-tuple-element.191, s32[]{:T(128)} %get-tuple-element.181, bf16[1,4,128,8,128]{4,3,2,1,0:T(8,128)(2,1)S(1)} %get-tuple-element.165), kind=kOutput, calls=%fused_computation.15.clone.1 | convolution fusion | flops 1073741824 | bytes 26214912 | tf_op jit(solution)/shard_map/while/body/eval_jaxpr/bqhd,bkhd->bhqk/dot_general | solution.py:104
  470.3 18.4 %fusion.80 = (f32[4,8,128]{2,1,0:T(8,128)S(1)}, f32[4,8,128,1024]{3,2,1,0:T(8,128)}) fusion(f32[4,8,128,1024]{3,2,1,0:T(8,128)} %fusion.79, pred[4,1024]{1,0:T(4,128)(4,1)S(1)} %dynamic-slice_bitcast_fusion.2), kind=kOutput, calls=%fused_computation.135.clone.1 | output fusion | flops 25166848 | bytes 33574912 | tf_op jit(solution)/shard_map/while/body/eval_jaxpr/sub | solution.py:108
  488.7 15.1 %multiply_reduce_fusion.6 = (f32[4,8,128]{2,1,0:T(8,128)S(1)}, f32[4,8,128,1024]{3,2,1,0:T(8,128)}) fusion(f32[4,8,128,1024]{3,2,1,0:T(8,128)} %get-tuple-element.166, f32[4,8,128]{2,1,0:T(8,128)S(1)} %get-tuple-element.167, bf16[2,4,1024,8,128]{2,4,3,1,0:T(8,128)(2,1)} %get-tuple-element.191, s32[]{:T(128)} %get-tuple-element.181, ...), kind=kOutput, calls=%fused_computation.6.clone.1 | convolution fusion | flops 1090514944 | bytes 43024896 | tf_op jit(solution)/shard_map/while/body/eval_jaxpr/bqhd,bkhd->bhqk/dot_general | solution.py:111
  503.8 29.9 %multiply_reduce_fusion.7 = (f32[4,8,128]{2,1,0:T(8,128)S(1)}, f32[4,8,128,1024]{3,2,1,0:T(8,128)}) fusion(f32[4,8,128,1024]{3,2,1,0:T(8,128)} %get-tuple-element.166, f32[4,8,128]{2,1,0:T(8,128)S(1)} %get-tuple-element.167, bf16[2,4,1024,8,128]{2,4,3,1,0:T(8,128)(2,1)} %get-tuple-element.194, s32[]{:T(128)} %get-tuple-element.181, ...), kind=kOutput, calls=%fused_computation.4.clone.1 | convolution fusion | flops 2181558272 | bytes 83952640 | tf_op jit(solution)/shard_map/while/body/eval_jaxpr/bqhd,bkhd->bhqk/dot_general | solution.py:119
  533.7 16.2 %bitcast_dynamic-update-slice_fusion.2 = f32[2,4,128,8,128]{2,4,3,1,0:T(8,128)} fusion(f32[2,4,128,8,128]{2,4,3,1,0:T(8,128)} %get-tuple-element.182, s32[]{:T(128)} %get-tuple-element.181, f32[4,8,128,1024]{3,2,1,0:T(8,128)} %get-tuple-element.171, f32[4,8,128]{2,1,0:T(8,128)S(1)} %get-tuple-element.172, ...), kind=kOutput, calls=%fused_computation.33.clone.1 | convolution fusion | flops 1091043328 | bytes 44073984 | tf_op jit(solution)/shard_map/while/body/eval_jaxpr/bhqk,bkhd->bqhd/dot_general | solution.py:125
  551.3 11.4 %fusion.79 = f32[4,8,128,1024]{3,2,1,0:T(8,128)} fusion(bf16[2,4,1024,8,128]{2,4,3,1,0:T(8,128)(2,1)} %get-tuple-element.191, s32[]{:T(128)} %get-tuple-element.181, bf16[1,4,128,8,128]{4,3,2,1,0:T(8,128)(2,1)S(1)} %get-tuple-element.165), kind=kOutput, calls=%fused_computation.15.clone.1 | convolution fusion | flops 1073741824 | bytes 26214912 | tf_op jit(solution)/shard_map/while/body/eval_jaxpr/bqhd,bkhd->bhqk/dot_general | solution.py:104
  562.7 18.4 %fusion.80 = (f32[4,8,128]{2,1,0:T(8,128)S(1)}, f32[4,8,128,1024]{3,2,1,0:T(8,128)}) fusion(f32[4,8,128,1024]{3,2,1,0:T(8,128)} %fusion.79, pred[4,1024]{1,0:T(4,128)(4,1)S(1)} %dynamic-slice_bitcast_fusion.2), kind=kOutput, calls=%fused_computation.135.clone.1 | output fusion | flops 25166848 | bytes 33574912 | tf_op jit(solution)/shard_map/while/body/eval_jaxpr/sub | solution.py:108
  581.1 15.1 %multiply_reduce_fusion.6 = (f32[4,8,128]{2,1,0:T(8,128)S(1)}, f32[4,8,128,1024]{3,2,1,0:T(8,128)}) fusion(f32[4,8,128,1024]{3,2,1,0:T(8,128)} %get-tuple-element.166, f32[4,8,128]{2,1,0:T(8,128)S(1)} %get-tuple-element.167, bf16[2,4,1024,8,128]{2,4,3,1,0:T(8,128)(2,1)} %get-tuple-element.191, s32[]{:T(128)} %get-tuple-element.181, ...), kind=kOutput, calls=%fused_computation.6.clone.1 | convolution fusion | flops 1090514944 | bytes 43024896 | tf_op jit(solution)/shard_map/while/body/eval_jaxpr/bqhd,bkhd->bhqk/dot_general | solution.py:111
  596.3 30.1 %multiply_reduce_fusion.7 = (f32[4,8,128]{2,1,0:T(8,128)S(1)}, f32[4,8,128,1024]{3,2,1,0:T(8,128)}) fusion(f32[4,8,128,1024]{3,2,1,0:T(8,128)} %get-tuple-element.166, f32[4,8,128]{2,1,0:T(8,128)S(1)} %get-tuple-element.167, bf16[2,4,1024,8,128]{2,4,3,1,0:T(8,128)(2,1)} %get-tuple-element.194, s32[]{:T(128)} %get-tuple-element.181, ...), kind=kOutput, calls=%fused_computation.4.clone.1 | convolution fusion | flops 2181558272 | bytes 83952640 | tf_op jit(solution)/shard_map/while/body/eval_jaxpr/bqhd,bkhd->bhqk/dot_general | solution.py:119
  626.4 16.2 %bitcast_dynamic-update-slice_fusion.2 = f32[2,4,128,8,128]{2,4,3,1,0:T(8,128)} fusion(f32[2,4,128,8,128]{2,4,3,1,0:T(8,128)} %get-tuple-element.182, s32[]{:T(128)} %get-tuple-element.181, f32[4,8,128,1024]{3,2,1,0:T(8,128)} %get-tuple-element.171, f32[4,8,128]{2,1,0:T(8,128)S(1)} %get-tuple-element.172, ...), kind=kOutput, calls=%fused_computation.33.clone.1 | convolution fusion | flops 1091043328 | bytes 44073984 | tf_op jit(solution)/shard_map/while/body/eval_jaxpr/bhqk,bkhd->bqhd/dot_general | solution.py:125
  657.3 39.9 %all-reduce = (f32[]{:T(128)}, f32[]{:T(128)}, f32[]{:T(128)}) all-reduce(f32[]{:T(128)} %multiply_reduce_fusion.3, f32[]{:T(128)} %get-tuple-element.62, f32[]{:T(128)} %get-tuple-element.61), channel_id=1, replica_groups=mesh['ctx'=8,'head'=4] {'ctx','head'}, use_global_device_ids=true, to_apply=%region_14.15 | all-reduce | flops 3 | bytes 24 | tf_op jit(solution)/shard_map/psum | solution.py:134
  701.7 7.0 fusion.47
  (61 shorter events, 57.5 us)
Async XLA Ops:
  27.6 7.4 %copy-start.1 = (s32[2]{0:T(128)S(1)}, s32[2]{0:T(128)}, u32[]{:S(2)}) copy-start(s32[2]{0:T(128)} %param.11) | copy-start | bytes 28
  27.6 340.9 %all-to-all-start = ((bf16[2,24,128,1024]{3,2,0,1:T(8,128)(2,1)}), bf16[2,24,128,1024]{3,2,0,1:T(8,128)(2,1)}, u32[]{:S(2)}, u32[]{:S(2)}) async-start(bf16[2,24,128,1024]{3,2,0,1:T(8,128)(2,1)} %select_bitcast_fusion), calls=%async_computation | async-start | bytes 25165824 | tf_op jit(solution)/shard_map/all_to_all | solution.py:74
  34.9 328.0 %all-reduce.4.cloned.1.call-start = ((), (), s32[]{:S(2)}) async-start(), calls=%async_computation.1 | async-start | bytes 2097152 | tf_op jit(solution)/shard_map/psum | solution.py:29
  41.2 112.2 %collective-permute-start = (bf16[2,128,1024]{2,1,0:T(8,128)(2,1)S(1)}, bf16[2,128,1024]{2,1,0:T(8,128)(2,1)}, u32[]{:S(2)}, u32[]{:S(2)}) collective-permute-start(bf16[2,128,1024]{2,1,0:T(8,128)(2,1)S(1)} %get-tuple-element.98), channel_id=1, source_target_pairs={{0,4},{4,8},{8,12},{12,16},{16,20},{20,24},{24,28},{1,5},{5,9},{9,... | collective-permute-start | bytes 1572872 | tf_op jit(solution)/shard_map/ppermute | solution.py:18
  45.8 107.5 %collective-permute-start.1 = (bf16[2,128,1024]{2,1,0:T(8,128)(2,1)S(1)}, bf16[2,128,1024]{2,1,0:T(8,128)(2,1)}, u32[]{:S(2)}, u32[]{:S(2)}) collective-permute-start(bf16[2,128,1024]{2,1,0:T(8,128)(2,1)S(1)} %get-tuple-element.97), channel_id=1, source_target_pairs={{4,0},{8,4},{12,8},{16,12},{20,16},{24,20},{28,24},{5,1},{9,5},{13... | collective-permute-start | bytes 1572872 | tf_op jit(solution)/shard_map/ppermute | solution.py:20
  55.4 104.1 %copy-start = (bf16[2,1024,1024]{2,1,0:T(8,128)(2,1)S(1)}, bf16[2,1024,1024]{2,1,0:T(8,128)(2,1)}, u32[]{:S(2)}) copy-start(bf16[2,1024,1024]{2,1,0:T(8,128)(2,1)} %param.8) | copy-start | bytes 12582916
Sparse Core Ops, SparseCore 0:
  47.3 315.6 all-reduce.3
where the time goes:
time: 718 us; the launch traced here: 716 us
  waiting for transfers between devices  293 us (41%)
  matrix products  146 us (20%)
  local copies, waits for them, and re-layouts  120 us (17%)
  other arithmetic  83.3 us (12%)
  blocking collectives  39.9 us (6%)
  between operations  21.1 us (3%)
  starting transfers between devices  13.3 us (2%)
    psum x1, waiting for transfers between devices, from_root(): return lax.psum(block, axis)  199 us
    ppermute x1, waiting for transfers between devices, padded_2(): lax.ppermute(tail, axis, [(i, (i + 1) % count) for i in range(ends)])  94.2 us
    dot_general x2, matrix products, attend(): jnp.einsum('bqhd,bkhd->bhqk', tangent_out, values, preferred_element_type...  60 us
    slice x2, local copies, waits for them, and re-layouts, local(): listed_kv[1].reshape(group_count, group_size, key_total, local_heads, HD)  44.6 us
    psum x1, blocking collectives, local(): lax.psum((jnp.sum(lanczos_vec * product), jnp.sum(product * product), jnp...  39.9 us
    sub x2, other arithmetic, attend(): weights = jnp.where(valid_wide, jnp.exp(scores - row_top), 0.0)  36.8 us
    dot_general x2, matrix products, attend(): jnp.einsum('bhqk,bkhd->bqhd', second_grad, key_part, preferred_element_ty...  32.4 us
    dot_general x2, matrix products, attend(): jnp.einsum('bqhd,bkhd->bhqk', tangent, key_part, preferred_element_type=j...  30.2 us
  transfers between devices with their start and end apart: 4, of which 2 were waited for; matrix products, arithmetic and copies ran while one was open for 4% of the time, Pallas kernels for 0%

commit v1 on v0

v1 whole, which is shorter than its diff:
```python
import functools

import jax
import jax.numpy as jnp
from jax import lax
from jax.experimental import pallas as pl
from jax.experimental.pallas import tpu as pltpu
from jax.sharding import PartitionSpec as P

HD = 128
BS = 128
SCALE = HD ** (-0.5)
LOG2E = 1.4426950408889634
NEG = float("-inf")
CHUNKS = 4
VMEM_LIMIT = 56 * 1024 * 1024


def attend(q, t, keys, vals, biases):
    k = jnp.concatenate(keys, axis=0)
    v = jnp.concatenate(vals, axis=0)
    nt = (((1,), (1,)), ((), ()))
    nn = (((1,), (0,)), ((), ()))
    both = lax.dot_general(
        jnp.concatenate([q, t.astype(jnp.bfloat16)], axis=0), k, nt,
        preferred_element_type=jnp.float32,
    )
    s = both[:BS]
    ds = both[BS:]
    parts = []
    for i in range(len(keys)):
        part = s[:, i * BS : (i + 1) * BS]
        parts.append(part if biases[i] is None else part + biases[i])
    s = jnp.concatenate(parts, axis=1)
    top = jnp.max(s, axis=1, keepdims=True)
    w = jnp.exp2((s - top) * (SCALE * LOG2E))
    inv = 1.0 / jnp.sum(w, axis=1, keepdims=True)
    p = w * inv
    center = jnp.sum(p * ds, axis=1, keepdims=True)
    g = ((p * SCALE) * (ds - center)).astype(jnp.bfloat16)
    dout = lax.dot_general(g, v, nn, preferred_element_type=jnp.float32).astype(jnp.bfloat16)
    dp = lax.dot_general(dout, v, nt, preferred_element_type=jnp.float32)
    center2 = jnp.sum(p * dp, axis=1, keepdims=True)
    g2 = (p * (dp - center2)).astype(jnp.bfloat16)
    return lax.dot_general(g2, k, nn, preferred_element_type=jnp.float32) * SCALE


def fold(x):
    return jnp.sum(x.reshape(BS // 8, 8, HD), axis=0)


def attend_kernel(nblocks, rand, slots, edge, q_ref, t_ref, kv_ref, lo_ref, hi_ref, gl_ref, in_ref, *rest):
    out_ref, sum_ref = rest[-2:]
    h = pl.program_id(0)

    @pl.when(h == 0)
    def _():
        sum_ref[...] = jnp.zeros_like(sum_ref)

    def block(b):
        rows = pl.ds(b * BS, BS)

        def listed(i):
            got = []
            if b == 0:
                got.append(lo_ref[i])
            else:
                got.append(kv_ref[i, (b - 1) * BS : b * BS, :])
            got.append(kv_ref[i, b * BS : (b + 1) * BS, :])
            if b == nblocks - 1:
                got.append(hi_ref[i])
            else:
                got.append(kv_ref[i, (b + 1) * BS : (b + 2) * BS, :])
            for g in range(gl_ref.shape[1] // BS):
                got.append(gl_ref[i, g * BS : (g + 1) * BS, :])
            for r in range(rand):
                got.append(in_ref[slots[b * rand + r], i])
            return got

        keys, vals = listed(0), listed(1)
        biases = [None] * len(keys)
        if b == 0:
            biases[0] = jnp.where(edge[0] > 0, NEG, 0.0).astype(jnp.float32)
        if b == nblocks - 1:
            biases[2] = jnp.where(edge[1] > 0, NEG, 0.0).astype(jnp.float32)
        t = t_ref[rows, :]
        image = attend(q_ref[rows, :], t, keys, vals, biases)
        out_ref[rows, :] = image
        sum_ref[0] += fold(t * image)
        sum_ref[1] += fold(image * image)
        sum_ref[2] += fold(t * t)

    for b in range(nblocks):
        block(b)


def attend_chunk(c, heads, queries, vec, key_value, lo, hi, glob, incoming, slots, edge, product):
    rows, width = queries.shape
    nblocks = rows // BS
    nslots = incoming.shape[0]
    rand = slots.shape[0] // nblocks
    first = c * heads
    col = lambda h, *_: (0, first + h)
    col3 = lambda h, *_: (0, 0, first + h)
    in_specs = [
        pl.BlockSpec((rows, HD), col),
        pl.BlockSpec((rows, HD), col),
        pl.BlockSpec((2, rows, HD), col3),
        pl.BlockSpec((2, BS, HD), col3),
        pl.BlockSpec((2, BS, HD), col3),
        pl.BlockSpec((2, glob.shape[1], HD), col3),
        pl.BlockSpec((nslots, 2, BS, HD), lambda h, *_: (0, 0, 0, h)),
    ]
    args = [slots, edge, queries, vec, key_value, lo, hi, glob, incoming]
    aliases = {}
    if product is not None:
        in_specs.append(pl.BlockSpec(memory_space=pl.ANY))
        aliases = {len(args): 0}
        args.append(product)
    return pl.pallas_call(
        functools.partial(attend_kernel, nblocks, rand),
        grid_spec=pltpu.PrefetchScalarGridSpec(
            num_scalar_prefetch=2,
            grid=(heads,),
            in_specs=in_specs,
            out_specs=[
                pl.BlockSpec((rows, HD), col),
                pl.BlockSpec((3, 8, HD), lambda h, *_: (0, 0, 0)),
            ],
        ),
        out_shape=[
            jax.ShapeDtypeStruct((rows, width), jnp.float32),
            jax.ShapeDtypeStruct((3, 8, HD), jnp.float32),
        ],
        input_output_aliases=aliases,
        compiler_params=pltpu.CompilerParams(vmem_limit_bytes=VMEM_LIMIT),
        cost_estimate=pl.CostEstimate(
            flops=heads * nblocks * 5 * 2 * BS * HD * 8 * BS * 4, bytes_accessed=heads * 8 * 2**20, transcendentals=0
        ),
    )(*args)


def pick_kernel(chosen, kv_ref, *outs):
    width = outs[0].shape[-1]
    for c, out in enumerate(outs):
        out[0] = kv_ref[:, :, c * width : (c + 1) * width]


def pick_blocks(key_value, chosen):
    count = chosen.shape[0]
    cols = key_value.shape[2]
    width = cols // CHUNKS
    return pl.pallas_call(
        pick_kernel,
        grid_spec=pltpu.PrefetchScalarGridSpec(
            num_scalar_prefetch=1,
            grid=(count,),
            in_specs=[pl.BlockSpec((2, BS, cols), lambda i, chosen: (0, chosen[i], 0))],
            out_specs=[pl.BlockSpec((1, 2, BS, width), lambda i, chosen: (i, 0, 0, 0))] * CHUNKS,
        ),
        out_shape=[jax.ShapeDtypeStruct((count, 2, BS, width), key_value.dtype)] * CHUNKS,
    )(chosen, key_value)


def from_root(block, axis, holder):
    block = jnp.where(lax.axis_index(axis) == holder, block, jnp.zeros_like(block))
    return lax.psum(block, axis)


def request_tables(rand_blocks, nblocks, ctx_count, ctx_index, capacity):
    requests = rand_blocks.reshape(ctx_count, -1)
    sources = requests // nblocks
    inside = requests % nblocks
    mine = (sources == ctx_index).astype(jnp.int32)
    earlier = jnp.cumsum(mine, axis=1) - mine
    slot_ids = jnp.arange(capacity, dtype=jnp.int32)
    matched = (mine[:, :, None] == 1) & (earlier[:, :, None] == slot_ids[None, None, :])
    chosen = jnp.sum(jnp.where(matched, inside[:, :, None], 0), axis=1).reshape(-1)
    own = lax.dynamic_index_in_dim(sources, ctx_index, 0, keepdims=False)
    total = own.shape[0]
    before = jnp.arange(total)[:, None] > jnp.arange(total)[None, :]
    same = own[:, None] == own[None, :]
    rank = jnp.sum((before & same).astype(jnp.int32), axis=1)
    return chosen, own * capacity + rank


def local(queries, key_value, lanczos_vec, rand_blocks, global_ids):
    rows, cols = queries.shape
    nblocks = rows // BS
    n = lax.axis_size("ctx")
    me = lax.axis_index("ctx")
    rand = rand_blocks.shape[1]
    capacity = (nblocks * rand + n - 1) // n
    chosen, slots = request_tables(rand_blocks, nblocks, n, me, capacity)
    outgoing = pick_blocks(key_value, chosen)
    incoming = [lax.all_to_all(part, "ctx", split_axis=0, concat_axis=0, tiled=True) for part in outgoing]
    lo = lax.ppermute(key_value[:, rows - BS :], "ctx", [(i, i + 1) for i in range(n - 1)])
    hi = lax.ppermute(key_value[:, :BS], "ctx", [(i + 1, i) for i in range(n - 1)])
    pieces = []
    for g in range(global_ids.shape[0]):
        piece = lax.dynamic_slice_in_dim(key_value, global_ids[g] % nblocks * BS, BS, 1)
        pieces.append(from_root(piece, "ctx", global_ids[g] // nblocks))
    glob = jnp.concatenate(pieces, axis=1)
    edge = jnp.stack([me == 0, me == n - 1]).astype(jnp.int32)
    product = None
    sums = 0.0
    heads = cols // HD // CHUNKS
    for c in range(CHUNKS):
        product, part = attend_chunk(
            c, heads, queries, lanczos_vec, key_value, lo, hi, glob, incoming[c], slots, edge, product
        )
        sums = sums + part
    count = float(rows * cols * n * lax.axis_size("head"))
    cross, image, vector = jnp.split(lax.psum(jnp.sum(sums, axis=(1, 2)), ("ctx", "head")), 3)
    alpha = cross[0] / count
    square = image[0] - 2.0 * alpha * cross[0] + alpha * alpha * vector[0]
    beta = jnp.sqrt(square / count + 1e-06)
    return (product - alpha * lanczos_vec) / beta, jnp.stack([alpha, beta])


def solution(mesh):
    placed = (P("ctx", "head"), P(None, "ctx", "head"), P("ctx", "head"), P(), P())
    return jax.shard_map(
        local, mesh=mesh, in_specs=placed, out_specs=(P("ctx", "head"), P()), check_vma=False
    )
```

time: 718 us -> 534 us (0.74)
  blocking collectives: 39.9 us -> 266 us
  waiting for transfers between devices: 293 us -> 114 us
  matrix products: 146 us -> 0 us
  local copies, waits for them, and re-layouts: 120 us -> 7.59 us
  Pallas kernels: 0 us -> 97.8 us
  other arithmetic: 83.3 us -> 13 us
    all_to_all x0 -> x3, blocking collectives: none -> 226 us  [local(): lax.all_to_all(part, 'ctx', split_axis=0, concat_axis=0, tiled=True)]
    dot_general x8 -> x0, matrix products: 146 us -> none  [the longest x2 60 us: attend(): jnp.einsum('bqhd,bkhd->bhqk', tangent_out, values, preferred_element_type...]
    pallas_call x0 -> x5, Pallas kernels: none -> 97.8 us  [the longest x4 79.2 us: attend_chunk(): pl.pallas_call(functools.partial(attend_kernel, nblocks, rand), grid_spec...]
    ppermute x2, waiting for transfers between devices: 94.2 us -> 0.01 us  [the longest x1 0.01 us: local(): lax.ppermute(key_value[:, rows - BS:], 'ctx', [(i, i + 1) for i in range(...]
    psum x1, waiting for transfers between devices: 199 us -> 114 us  [from_root(): return lax.psum(block, axis)]
    slice x4 -> x1, local copies, waits for them, and re-layouts: 66.8 us -> 0.58 us  [local(): pieces.append(from_root(piece, 'ctx', global_ids[g] // nblocks))]
    sub x3 -> x1, other arithmetic: 36.9 us -> 0.01 us  [request_tables(): earlier = jnp.cumsum(mine, axis=1) - mine]
    gather x3 -> x0, local copies, waits for them, and re-layouts: 25.2 us -> none  [the longest x2 17 us: local(): random_kv = jnp.take(incoming, own_sources * capacity + order_rank, axis=1)]
  transfers between devices with their start and end apart: 4 -> 4, of which waited for: 2 -> 1; matrix products, arithmetic and copies ran while one was open for 4% -> 1% of each run, Pallas kernels for 0% -> 11%
where the time goes in v1:
time: 534 us; the launch traced here: 532 us
  blocking collectives  266 us (50%)
  waiting for transfers between devices  114 us (21%)
  Pallas kernels  97.8 us (18%)
  between operations  23.8 us (4%)
  other arithmetic  13 us (2%)
  starting transfers between devices  10.5 us (2%)
  local copies, waits for them, and re-layouts  7.59 us (1%)
    all_to_all x3, blocking collectives, local(): lax.all_to_all(part, 'ctx', split_axis=0, concat_axis=0, tiled=True)  226 us
    psum x1, waiting for transfers between devices, from_root(): return lax.psum(block, axis)  114 us
    pallas_call x4, Pallas kernels, attend_chunk(): pl.pallas_call(functools.partial(attend_kernel, nblocks, rand), grid_spec...  79.2 us
    psum x1, blocking collectives, local(): lax.psum(jnp.sum(sums, axis=(1, 2)), ('ctx', 'head'))  39.6 us
    pallas_call x1, Pallas kernels, pick_blocks(): pl.pallas_call(pick_kernel, grid_spec=pltpu.PrefetchScalarGridSpec(num_sc...  18.6 us
  transfers between devices with their start and end apart: 4, of which 1 were waited for; matrix products, arithmetic and copies ran while one was open for 1% of the time, Pallas kernels for 11%

profile of v1, /device:TPU:0, one launch (start us, length us, event | category | flops | bytes accessed | tf_op | source)
XLA Modules:
  0.0 532.5 jit_solution(1496847215978438047)
XLA Ops:
  7.2 0.8 copy.12
  8.5 0.6 reshape.111.chosen
  9.1 18.6 %shard_map.68 = (bf16[24,2,128,256]{3,2,1,0:T(8,128)(2,1)}, bf16[24,2,128,256]{3,2,1,0:T(8,128)(2,1)}, bf16[24,2,128,256]{3,2,1,0:T(8,128)(2,1)}, bf16[24,2,128,256]{3,2,1,0:T(8,128)(2,1)}) custom-call(s32[24]{0:T(128)} %reshape.111.chosen, bf16[2,1024,1024]{2,1,0:T(8,128)(2,1)} %kv_ref.9), custom_call_target="tpu_custom_call" | custom-call | tf_op jit(solution)/shard_map/pallas_call | solution.py:153
  27.6 78.0 %all_to_all.20.in_ref = bf16[24,2,128,256]{3,2,1,0:T(8,128)(2,1)} all-to-all(bf16[24,2,128,256]{3,2,1,0:T(8,128)(2,1)} %get-tuple-element.15), channel_id=1, replica_groups=mesh['ctx'=8,'head'=4] {'ctx'}, dimensions={0} | all-to-all | bytes 6291456 | tf_op jit(solution)/shard_map/all_to_all | solution.py:196
  105.7 74.2 %all_to_all.21.in_ref = bf16[24,2,128,256]{3,2,1,0:T(8,128)(2,1)} all-to-all(bf16[24,2,128,256]{3,2,1,0:T(8,128)(2,1)S(1)} %copy-done.2), channel_id=1, replica_groups=mesh['ctx'=8,'head'=4] {'ctx'}, dimensions={0} | all-to-all | bytes 6291456 | tf_op jit(solution)/shard_map/all_to_all | solution.py:196
  179.9 73.7 %all_to_all.22.in_ref = bf16[24,2,128,256]{3,2,1,0:T(8,128)(2,1)} all-to-all(bf16[24,2,128,256]{3,2,1,0:T(8,128)(2,1)S(1)} %copy-done.1), channel_id=1, replica_groups=mesh['ctx'=8,'head'=4] {'ctx'}, dimensions={0} | all-to-all | bytes 6291456 | tf_op jit(solution)/shard_map/all_to_all | solution.py:196
  253.6 3.8 all-to-all-start
  263.3 3.0 dynamic-slice_select_fusion
  266.3 1.3 collective-permute-start.1
  267.6 5.4 %collective-permute-start = (bf16[2,128,1024]{2,1,0:T(8,128)(2,1)}, bf16[2,128,1024]{2,1,0:T(8,128)(2,1)}, u32[]{:S(2)}, u32[]{:S(2)}) collective-permute-start(bf16[2,128,1024]{2,1,0:T(8,128)(2,1)} %get-tuple-element.33), channel_id=1, source_target_pairs={{0,4},{4,8},{8,12},{12,16},{16,20},{20,24},{24,28},{1,5},{5,9},{9,... | collective-permute-start | bytes 1572872 | tf_op jit(solution)/shard_map/ppermute | solution.py:197
  274.2 114.2 %all-reduce.3.cloned.1.call-done = (bf16[2,128,1024]{2,1,0:T(8,128)(2,1)}, bf16[2,128,1024]{2,1,0:T(8,128)(2,1)}) async-done(((bf16[2,128,1024]{2,1,0:T(8,128)(2,1)}, bf16[2,128,1024]{2,1,0:T(8,128)(2,1)}), (bf16[2,128,1024]{2,1,0:T(8,128)(2,1)}, bf16[2,128,1024]{2,1,0:T(8,128)(2,1)})) %all-reduce.3.cloned.1.call-update) | async-done | bytes 1048592 | tf_op jit(solution)/shard_map/psum | solution.py:167
  388.5 1.1 constant_dynamic-update-slice_fusion.1
  389.6 1.1 constant_dynamic-update-slice_fusion.gl_ref
  390.7 1.0 copy-done.3
  391.7 19.7 %shard_map.69 = (f32[1024,1024]{1,0:T(8,128)}, f32[3,8,128]{2,1,0:T(8,128)}) custom-call(s32[24]{0:T(128)} %multiply_add_fusion.slots, s32[2]{0:T(128)} %add_convert_fusion.edge, bf16[1024,1024]{1,0:T(8,128)(2,1)} %q_ref.7, f32[1024,1024]{1,0:T(8,128)} %t_ref.7, bf16[2,1024,1024]{2,1,0:T(8,128)(2,1)} %kv_ref.9, ...), custom_call_target="tpu_custom_call" | custom-call | flops 10737418240 | bytes 16777216 | tf_op jit(solution)/shard_map/pallas_call | solution.py:120
  411.4 19.7 %shard_map.70 = (f32[1024,1024]{1,0:T(8,128)}, f32[3,8,128]{2,1,0:T(8,128)}) custom-call(s32[24]{0:T(128)} %multiply_add_fusion.slots, s32[2]{0:T(128)} %add_convert_fusion.edge, bf16[1024,1024]{1,0:T(8,128)(2,1)} %q_ref.7, f32[1024,1024]{1,0:T(8,128)} %t_ref.7, bf16[2,1024,1024]{2,1,0:T(8,128)(2,1)} %kv_ref.9, ...), custom_call_target="tpu_custom_call", output_to_operand_aliasing={{0}: (9, {})} | custom-call | flops 10737418240 | bytes 16777216 | tf_op jit(solution)/shard_map/pallas_call | solution.py:120
  431.1 19.9 %shard_map.71 = (f32[1024,1024]{1,0:T(8,128)}, f32[3,8,128]{2,1,0:T(8,128)}) custom-call(s32[24]{0:T(128)} %multiply_add_fusion.slots, s32[2]{0:T(128)} %add_convert_fusion.edge, bf16[1024,1024]{1,0:T(8,128)(2,1)} %q_ref.7, f32[1024,1024]{1,0:T(8,128)} %t_ref.7, bf16[2,1024,1024]{2,1,0:T(8,128)(2,1)} %kv_ref.9, ...), custom_call_target="tpu_custom_call", output_to_operand_aliasing={{0}: (9, {})} | custom-call | flops 10737418240 | bytes 16777216 | tf_op jit(solution)/shard_map/pallas_call | solution.py:120
  451.1 1.6 copy-done
  452.7 19.9 %shard_map.72 = (f32[1024,1024]{1,0:T(8,128)}, f32[3,8,128]{2,1,0:T(8,128)}) custom-call(s32[24]{0:T(128)} %multiply_add_fusion.slots, s32[2]{0:T(128)} %add_convert_fusion.edge, bf16[1024,1024]{1,0:T(8,128)(2,1)} %q_ref.7, f32[1024,1024]{1,0:T(8,128)} %t_ref.7, bf16[2,1024,1024]{2,1,0:T(8,128)(2,1)} %kv_ref.9, ...), custom_call_target="tpu_custom_call", output_to_operand_aliasing={{0}: (9, {})} | custom-call | flops 10737418240 | bytes 16777216 | tf_op jit(solution)/shard_map/pallas_call | solution.py:120
  472.6 0.8 add_reduce_fusion
  473.4 39.6 %psum.23 = f32[3]{0:T(128)S(1)} all-reduce(f32[3]{0:T(128)S(1)} %add_reduce_fusion), channel_id=1, replica_groups=mesh['ctx'=8,'head'=4] {'ctx','head'}, use_global_device_ids=true, to_apply=%region_6.7 | all-reduce | flops 3 | bytes 24 | tf_op jit(solution)/shard_map/psum | solution.py:214
  513.0 0.6 fusion.5
  518.1 7.0 %subtract_divide_fusion = f32[1024,1024]{1,0:T(8,128)} fusion(f32[1024,1024]{1,0:T(8,128)} %get-tuple-element.21, f32[1024,1024]{1,0:T(8,128)} %t_ref.7, f32[]{:T(128)} %sqrt.3, f32[]{:T(128)} %div.49), kind=kLoop, calls=%fused_computation | loop fusion | flops 3145728 | bytes 12582920 | tf_op jit(solution)/shard_map/div | solution.py:218
  525.1 0.6 pad_maximum_fusion
  (31 shorter events, 2.5 us)
Async XLA Ops:
  27.6 78.0 %copy-start.2 = (bf16[24,2,128,256]{3,2,1,0:T(8,128)(2,1)S(1)}, bf16[24,2,128,256]{3,2,1,0:T(8,128)(2,1)}, u32[]{:S(2)}) copy-start(bf16[24,2,128,256]{3,2,1,0:T(8,128)(2,1)} %get-tuple-element.16) | copy-start | bytes 9437188
  105.7 74.2 %copy-start.1 = (bf16[24,2,128,256]{3,2,1,0:T(8,128)(2,1)S(1)}, bf16[24,2,128,256]{3,2,1,0:T(8,128)(2,1)}, u32[]{:S(2)}) copy-start(bf16[24,2,128,256]{3,2,1,0:T(8,128)(2,1)} %get-tuple-element.17) | copy-start | bytes 9437188
  253.6 3.8 copy-start.7
  253.6 197.4 %all-to-all-start = ((bf16[24,2,128,256]{3,2,1,0:T(8,128)(2,1)}), bf16[24,2,128,256]{3,2,1,0:T(8,128)(2,1)S(1)}, u32[]{:S(2)}, u32[]{:S(2)}) async-start(bf16[24,2,128,256]{3,2,1,0:T(8,128)(2,1)} %get-tuple-element.14), calls=%async_computation | async-start | bytes 6291456 | tf_op jit(solution)/shard_map/all_to_all | solution.py:196
  257.4 131.1 %all-reduce.3.cloned.1.call-start = ((), (), s32[]{:S(2)}) async-start(), calls=%async_computation.4 | async-start | bytes 2097152 | tf_op jit(solution)/shard_map/psum | solution.py:167
  266.3 124.4 %collective-permute-start.1 = (bf16[2,128,1024]{2,1,0:T(8,128)(2,1)}, bf16[2,128,1024]{2,1,0:T(8,128)(2,1)}, u32[]{:S(2)}, u32[]{:S(2)}) collective-permute-start(bf16[2,128,1024]{2,1,0:T(8,128)(2,1)} %get-tuple-element.32), channel_id=1, source_target_pairs={{4,0},{8,4},{12,8},{16,12},{20,16},{24,20},{28,24},{5,1},{9,5},{13... | collective-permute-start | bytes 1572872 | tf_op jit(solution)/shard_map/ppermute | solution.py:198
  267.6 123.1 %collective-permute-start = (bf16[2,128,1024]{2,1,0:T(8,128)(2,1)}, bf16[2,128,1024]{2,1,0:T(8,128)(2,1)}, u32[]{:S(2)}, u32[]{:S(2)}) collective-permute-start(bf16[2,128,1024]{2,1,0:T(8,128)(2,1)} %get-tuple-element.33), channel_id=1, source_target_pairs={{0,4},{4,8},{8,12},{12,16},{16,20},{20,24},{24,28},{1,5},{5,9},{9,... | collective-permute-start | bytes 1572872 | tf_op jit(solution)/shard_map/ppermute | solution.py:197
  390.6 1.0 copy-start.3
  451.1 1.6 copy-start
  452.7 19.9 %copy-start.4 = (f32[3,8,128]{2,1,0:T(8,128)S(1)}, f32[3,8,128]{2,1,0:T(8,128)}, u32[]{:S(2)}) copy-start(f32[3,8,128]{2,1,0:T(8,128)} %get-tuple-element.22) | copy-start | bytes 36868
  452.7 19.9 %copy-start.5 = (f32[3,8,128]{2,1,0:T(8,128)S(1)}, f32[3,8,128]{2,1,0:T(8,128)}, u32[]{:S(2)}) copy-start(f32[3,8,128]{2,1,0:T(8,128)} %get-tuple-element.23) | copy-start | bytes 36868
  452.7 19.9 %copy-start.6 = (f32[3,8,128]{2,1,0:T(8,128)S(1)}, f32[3,8,128]{2,1,0:T(8,128)}, u32[]{:S(2)}) copy-start(f32[3,8,128]{2,1,0:T(8,128)} %get-tuple-element.24) | copy-start | bytes 36868
Sparse Core Ops, SparseCore 0:
  266.4 122.0 all-reduce.2

commit v2 on v1

--- a/solution.py
+++ b/solution.py
@@ -14,6 +14,9 @@
 NEG = float("-inf")
 CHUNKS = 4
 VMEM_LIMIT = 56 * 1024 * 1024
+NZ = 4
+NY = 2
+MESH = pl.DeviceIdType.MESH
 
 
 def attend(q, t, keys, vals, biases):
@@ -210,16 +213,381 @@
             c, heads, queries, lanczos_vec, key_value, lo, hi, glob, incoming[c], slots, edge, product
         )
         sums = sums + part
-    count = float(rows * cols * n * lax.axis_size("head"))
-    cross, image, vector = jnp.split(lax.psum(jnp.sum(sums, axis=(1, 2)), ("ctx", "head")), 3)
-    alpha = cross[0] / count
-    square = image[0] - 2.0 * alpha * cross[0] + alpha * alpha * vector[0]
+    totals = lax.psum(jnp.sum(sums, axis=(1, 2)), ("ctx", "head"))
+    return finish(product, lanczos_vec, totals, float(rows * cols * n * lax.axis_size("head")))
+
+
+def finish(product, vec, totals, count):
+    cross, image, vector = totals[0], totals[1], totals[2]
+    alpha = cross / count
+    square = image - 2.0 * alpha * cross + alpha * alpha * vector
     beta = jnp.sqrt(square / count + 1e-06)
-    return (product - alpha * lanczos_vec) / beta, jnp.stack([alpha, beta])
+    return (product - alpha * vec) / beta, jnp.stack([alpha, beta])
+
+
+def line_kernel(dims, tab, q_ref, t_ref, kv_ref, out_ref, sum_ref, *scratch):
+    nb, heads, rand, nglob, cap, keep, nctx, nhead = dims
+    rowbufs = scratch[:heads]
+    ybufs = scratch[heads : 2 * heads]
+    (pool, ysend, left_order, glbuf, halo, red1, red2, right_s, right_r, left_s, left_r,
+     y_s, y_r, gl_s, gl_r, halo_s, halo_r, red_s, red_r) = scratch[2 * heads :]
+    ny_slots = NZ * cap
+    o_right, o_left = 0, nb
+    o_y = 2 * nb
+    o_g = o_y + ny_slots
+    o_gl = o_g + nglob
+    o_r = o_gl + nglob
+    me = lax.axis_index("ctx")
+    hd = lax.axis_index("head")
+    z = me // NY
+    y = me % NY
+    peer = z * NY + (NY - 1 - y)
+    last = NZ - 1
+
+    barrier = pltpu.get_barrier_semaphore()
+    for o in range(1, nctx):
+        pl.semaphore_signal(barrier, inc=1, device_id={"ctx": lax.rem(me + o, nctx)}, device_id_type=MESH)
+    for o in range(1, nhead):
+        pl.semaphore_signal(barrier, inc=1, device_id={"head": lax.rem(hd + o, nhead)}, device_id_type=MESH)
+
+    def cols(c):
+        return slice(c * HD, (c + 1) * HD)
+
+    def hop(c, right, s, count):
+        pos_z = z - s if right else z + s
+        place = pl.ds(pos_z * nb, count)
+        target = me + NY if right else me - NY
+        if s == 0 and not right:
+            source = left_order.at[c % 2, pl.ds(0, count)]
+        else:
+            source = rowbufs[c].at[place]
+        ss, rr = (right_s, right_r) if right else (left_s, left_r)
+        return pltpu.make_async_remote_copy(
+            src_ref=source, dst_ref=rowbufs[c].at[place], send_sem=ss.at[c, s], recv_sem=rr.at[c, s],
+            device_id={"ctx": target}, device_id_type=MESH,
+        )
+
+    def each_hop(c, right, s, act):
+        pos = z if right else last - z
+
+        @pl.when((pos >= s) & (pos < last - 1))
+        def _():
+            act(hop(c, right, s, nb))
+
+        @pl.when(pos == last - 1)
+        def _():
+            if s <= last - 1:
+                act(hop(c, right, s, keep))
+
+    def arrive(c, right, s):
+        pos = z if right else last - z
+        src_z = z - s - 1 if right else z + s + 1
+        ss, rr = (right_s, right_r) if right else (left_s, left_r)
+
+        def wait(count):
+            place = rowbufs[c].at[pl.ds(src_z * nb, count)]
+            pltpu.make_async_remote_copy(
+                src_ref=place, dst_ref=place, send_sem=ss.at[c, s], recv_sem=rr.at[c, s],
+                device_id={"ctx": peer}, device_id_type=MESH,
+            ).wait_recv()
+
+        @pl.when((pos >= s + 1) & (pos < last))
+        def _():
+            wait(nb)
+
+        @pl.when(pos == last)
+        def _():
+            wait(keep)
+
+    def halo_copy(c, up):
+        block = nb - 1 if up else 0
+        i = 0 if up else 1
+        return pltpu.make_async_remote_copy(
+            src_ref=kv_ref.at[:, block, :, cols(c)], dst_ref=halo.at[c, i],
+            send_sem=halo_s.at[c, i], recv_sem=halo_r.at[c, i],
+            device_id={"ctx": me + 1 if up else me - 1}, device_id_type=MESH,
+        )
+
+    def y_copy(c):
+        return pltpu.make_async_remote_copy(
+            src_ref=ysend.at[c % 2], dst_ref=ybufs[c], send_sem=y_s.at[c], recv_sem=y_r.at[c],
+            device_id={"ctx": peer}, device_id_type=MESH,
+        )
+
+    def gl_copy(c, right):
+        return pltpu.make_async_remote_copy(
+            src_ref=ysend.at[c % 2, pl.ds(ny_slots, nglob)], dst_ref=glbuf.at[c],
+            send_sem=gl_s.at[c], recv_sem=gl_r.at[c],
+            device_id={"ctx": me + NY if right else me - NY}, device_id_type=MESH,
+        )
+
+    def each_gl(c, act):
+        @pl.when(z == last - 1)
+        def _():
+            act(gl_copy(c, True))
+
+        @pl.when(z == 1)
+        def _():
+            act(gl_copy(c, False))
+
+    def own_left_sent(c):
+        each_hop(c, False, 0, lambda copy: copy.wait_send())
+
+    def begin(c):
+        if c >= 2:
+            own_left_sent(c - 2)
+        for i in range(nb):
+            rowbufs[c][z * nb + i] = kv_ref[:, tab[o_right + i], :, cols(c)]
+            left_order[c % 2, i] = kv_ref[:, tab[o_left + i], :, cols(c)]
+        each_hop(c, True, 0, lambda copy: copy.start())
+        each_hop(c, False, 0, lambda copy: copy.start())
+
+        @pl.when(me < nctx - 1)
+        def _():
+            halo_copy(c, True).start()
+
+        @pl.when(me > 0)
+        def _():
+            halo_copy(c, False).start()
+
+        @pl.when(me == 0)
+        def _():
+            halo[c, 0] = jnp.zeros(halo.shape[2:], halo.dtype)
+
+        @pl.when(me == nctx - 1)
+        def _():
+            halo[c, 1] = jnp.zeros(halo.shape[2:], halo.dtype)
+
+    def relay(c, s):
+        arrive(c, True, s - 1)
+        arrive(c, False, s - 1)
+        if s < last:
+            each_hop(c, True, s, lambda copy: copy.start())
+            each_hop(c, False, s, lambda copy: copy.start())
+
+    def across(c):
+        if c >= 2:
+            y_copy(c - 2).wait_send()
+            each_gl(c - 2, lambda copy: copy.wait_send())
+        pool[: NZ * nb] = rowbufs[c][...]
+
+        @pl.when((z == 0) | (z == last))
+        def _():
+            gl_copy(c, True).wait_recv()
+            pool[NZ * nb + ny_slots + nglob :] = glbuf[c]
+
+        for g in range(nglob):
+            ysend[c % 2, ny_slots + g] = pool[tab[o_g + g]]
+        each_gl(c, lambda copy: copy.start())
+        for i in range(ny_slots):
+            ysend[c % 2, i] = pool[tab[o_y + i]]
+        y_copy(c).start()
+
+    def compute(c):
+        y_copy(c).wait_recv()
+        pool[NZ * nb : NZ * nb + ny_slots + nglob] = ybufs[c][...]
+
+        @pl.when(me > 0)
+        def _():
+            halo_copy(c, True).wait_recv()
+
+        @pl.when(me < nctx - 1)
+        def _():
+            halo_copy(c, False).wait_recv()
+
+        def body(b, carry):
+            def own(i):
+                return kv_ref[:, i, :, cols(c)]
+
+            got = [
+                lax.select(b == 0, halo[c, 0], own(jnp.maximum(b - 1, 0))),
+                own(b),
+                lax.select(b == nb - 1, halo[c, 1], own(jnp.minimum(b + 1, nb - 1))),
+            ]
+            for g in range(nglob):
+                got.append(pool[tab[o_gl + g]])
+            for r in range(rand):
+                got.append(pool[tab[o_r + b * rand + r]])
+            biases = [None] * len(got)
+            biases[0] = jnp.where((b == 0) & (me == 0), NEG, 0.0).astype(jnp.float32)
+            biases[2] = jnp.where((b == nb - 1) & (me == nctx - 1), NEG, 0.0).astype(jnp.float32)
+            rows = pl.ds(pl.multiple_of(b * BS, BS), BS)
+            t = t_ref[rows, cols(c)]
+            image = attend(q_ref[rows, cols(c)], t, [x[0] for x in got], [x[1] for x in got], biases)
+            out_ref[rows, cols(c)] = image
+            sum_ref[0] += fold(t * image)
+            sum_ref[1] += fold(image * image)
+            sum_ref[2] += fold(t * t)
+            return carry
+
+        lax.fori_loop(0, nb, body, 0)
+
+    pl.semaphore_wait(barrier, nctx - 1 + nhead - 1)
+    sum_ref[...] = jnp.zeros_like(sum_ref)
+    begin(0)
+    for c in range(heads):
+        if c + 1 < heads:
+            begin(c + 1)
+        relay(c, 1)
+        if c >= 1:
+            compute(c - 1)
+        relay(c, 2)
+        relay(c, 3)
+        across(c)
+    compute(heads - 1)
+
+    def share(buf, axis, mine, count, base):
+        buf[mine] = sum_ref[...]
+        copies = []
+        for o in range(1, count):
+            copy = pltpu.make_async_remote_copy(
+                src_ref=buf.at[mine], dst_ref=buf.at[mine],
+                send_sem=red_s.at[base + o - 1], recv_sem=red_r.at[base + o - 1],
+                device_id={axis: lax.rem(mine + o, count)}, device_id_type=MESH,
+            )
+            copy.start()
+            copies.append(copy)
+        for o in range(1, count):
+            place = buf.at[lax.rem(mine + count - o, count)]
+            pltpu.make_async_remote_copy(
+                src_ref=place, dst_ref=place,
+                send_sem=red_s.at[base + o - 1], recv_sem=red_r.at[base + o - 1],
+                device_id={axis: lax.rem(mine + o, count)}, device_id_type=MESH,
+            ).wait_recv()
+        total = buf[0]
+        for i in range(1, count):
+            total = total + buf[i]
+        sum_ref[...] = total
+        for copy in copies:
+            copy.wait_send()
+
+    share(red1, "head", hd, nhead, 0)
+    share(red2, "ctx", me, nctx, nhead - 1)
+
+    for c in range(heads):
+        for s in range(last):
+            each_hop(c, True, s, lambda copy: copy.wait_send())
+            if s > 0 or c >= heads - 2:
+                each_hop(c, False, s, lambda copy: copy.wait_send())
+
+        @pl.when(me < nctx - 1)
+        def _():
+            halo_copy(c, True).wait_send()
+
+        @pl.when(me > 0)
+        def _():
+            halo_copy(c, False).wait_send()
+
+        if c >= heads - 2:
+            y_copy(c).wait_send()
+            each_gl(c, lambda copy: copy.wait_send())
+
+
+def line_tables(rand_blocks, global_ids, nb, me, cap, keep):
+    n = NZ * NY
+    z, y = me // NY, me % NY
+    requests = rand_blocks.reshape(n, -1)
+    wanted = (requests[:, None, :] == jnp.arange(n * nb, dtype=jnp.int32)[None, :, None]).any(axis=2)
+    layer = wanted.reshape(NZ, NY, n * nb).any(axis=1)
+
+    def order(need):
+        need = need.reshape(n, nb).astype(jnp.int32)
+        first = jnp.cumsum(need, axis=1)
+        rest = jnp.cumsum(1 - need, axis=1)
+        rank = jnp.where(need == 1, first - 1, first[:, -1:] + rest - 1)
+        return rank
+
+    rank_r = order(layer[NZ - 1])
+    rank_l = order(layer[0])
+    ids = jnp.arange(nb, dtype=jnp.int32)
+
+    def inverse(rank):
+        mine = lax.dynamic_index_in_dim(rank, me, 0, keepdims=False)
+        return jnp.sum(jnp.where(mine[None, :] == ids[:, None], ids[None, :], 0), axis=1)
+
+    src_z = jnp.arange(n, dtype=jnp.int32) // NY
+    rank = jnp.where((src_z <= z)[:, None], rank_r, rank_l)
+    place = (src_z[:, None] * nb + rank).reshape(-1)
+
+    def lookup(blocks):
+        hit = blocks[:, None] == jnp.arange(n * nb, dtype=jnp.int32)[None, :]
+        return jnp.sum(jnp.where(hit, place[None, :], 0), axis=1)
+
+    def ranks(req):
+        source = req // nb
+        total = req.shape[0]
+        before = jnp.arange(total)[:, None] > jnp.arange(total)[None, :]
+        return jnp.sum((before & (source[:, None] == source[None, :])).astype(jnp.int32), axis=1)
+
+    own = lax.dynamic_index_in_dim(requests, me, 0, keepdims=False)
+    other = lax.dynamic_index_in_dim(requests, z * NY + (NY - 1 - y), 0, keepdims=False)
+    other_src = other // nb
+    other_slot = jnp.where(other_src % NY == y, (other_src // NY) * cap + ranks(other), -1)
+    slot = jnp.arange(NZ * cap, dtype=jnp.int32)
+    y_src = jnp.sum(jnp.where(other_slot[None, :] == slot[:, None], lookup(other)[None, :], 0), axis=1)
+    g_owner = global_ids // nb
+    g_ids = jnp.arange(global_ids.shape[0], dtype=jnp.int32)
+    far = ((z == 0) | (z == NZ - 1)) & (g_owner // NY != z)
+    y_base = NZ * nb
+    g_base = y_base + NZ * cap
+    g_src = jnp.where(far, g_base + g_ids.shape[0] + g_ids, lookup(global_ids))
+    g_all = jnp.where(g_owner % NY == y, g_src, g_base + g_ids)
+    own_src = own // nb
+    r_all = jnp.where(own_src % NY == y, lookup(own), y_base + (own_src // NY) * cap + ranks(own))
+    parts = [inverse(rank_r), inverse(rank_l), y_src, g_src, g_all, r_all]
+    return jnp.concatenate([p.astype(jnp.int32) for p in parts])
+
+
+def line_local(queries, key_value, lanczos_vec, rand_blocks, global_ids):
+    rows, cols = queries.shape
+    nb = rows // BS
+    heads = cols // HD
+    n = lax.axis_size("ctx")
+    nhead = lax.axis_size("head")
+    me = lax.axis_index("ctx")
+    rand = rand_blocks.shape[1]
+    nglob = global_ids.shape[0]
+    cap = (nb * rand + n - 1) // n
+    keep = min(nb, NY * cap)
+    tab = line_tables(rand_blocks, global_ids, nb, me, cap, keep)
+    slots = NZ * cap + nglob
+    dims = (nb, heads, rand, nglob, cap, keep, n, nhead)
+    unit = (2, BS, HD)
+    vmem = pl.BlockSpec(memory_space=pltpu.VMEM)
+    sem = pltpu.SemaphoreType.DMA
+    product, sums = pl.pallas_call(
+        functools.partial(line_kernel, dims),
+        in_specs=[pl.BlockSpec(memory_space=pltpu.SMEM), vmem, vmem, vmem],
+        out_specs=[vmem, vmem],
+        out_shape=[
+            jax.ShapeDtypeStruct((rows, cols), jnp.float32),
+            jax.ShapeDtypeStruct((3, 8, HD), jnp.float32),
+        ],
+        scratch_shapes=[pltpu.VMEM((NZ * nb,) + unit, jnp.bfloat16)] * heads
+        + [pltpu.VMEM((slots,) + unit, jnp.bfloat16)] * heads
+        + [
+            pltpu.VMEM((NZ * nb + slots + nglob,) + unit, jnp.bfloat16),
+            pltpu.VMEM((2, slots) + unit, jnp.bfloat16),
+            pltpu.VMEM((2, nb) + unit, jnp.bfloat16),
+            pltpu.VMEM((heads, nglob) + unit, jnp.bfloat16),
+            pltpu.VMEM((heads, 2) + unit, jnp.bfloat16),
+            pltpu.VMEM((nhead, 3, 8, HD), jnp.float32),
+            pltpu.VMEM((n, 3, 8, HD), jnp.float32),
+            sem((heads, NZ)), sem((heads, NZ)), sem((heads, NZ)), sem((heads, NZ)),
+            sem((heads,)), sem((heads,)), sem((heads,)), sem((heads,)),
+            sem((heads, 2)), sem((heads, 2)),
+            sem((n + nhead,)), sem((n + nhead,)),
+        ],
+        compiler_params=pltpu.CompilerParams(
+            collective_id=0, has_side_effects=True, vmem_limit_bytes=VMEM_LIMIT
+        ),
+    )(tab, queries, lanczos_vec, key_value.reshape(2, nb, BS, cols))
+    return finish(product, lanczos_vec, jnp.sum(sums, axis=(1, 2)), float(rows * cols * n * nhead))
 
 
 def solution(mesh):
     placed = (P("ctx", "head"), P(None, "ctx", "head"), P("ctx", "head"), P(), P())
+    body = line_local if mesh.shape["ctx"] == NZ * NY else local
     return jax.shard_map(
-        local, mesh=mesh, in_specs=placed, out_specs=(P("ctx", "head"), P()), check_vma=False
+        body, mesh=mesh, in_specs=placed, out_specs=(P("ctx", "head"), P()), check_vma=False
     )

time: 534 us -> 318 us (0.60)
  blocking collectives: 266 us -> 0 us
  Pallas kernels: 97.8 us -> 297 us
  waiting for transfers between devices: 114 us -> 0 us
  between operations: 23.8 us -> 5.13 us
  starting transfers between devices: 10.5 us -> 0 us
    all_to_all x3 -> x0, blocking collectives: 226 us -> none  [local(): lax.all_to_all(part, 'ctx', split_axis=0, concat_axis=0, tiled=True)]
    pallas_call x5 -> x1, Pallas kernels: 97.8 us -> 297 us  [line_local(): pl.pallas_call(functools.partial(line_kernel, dims), in_specs=[pl.BlockSp...]
    psum x1 -> x0, waiting for transfers between devices: 114 us -> none  [from_root(): return lax.psum(block, axis)]
    psum x1 -> x0, blocking collectives: 39.6 us -> none  [local(): lax.psum(jnp.sum(sums, axis=(1, 2)), ('ctx', 'head'))]
    ppermute x2 -> x0, starting transfers between devices: 6.65 us -> none  [the longest x1 5.36 us: local(): lax.ppermute(key_value[:, rows - BS:], 'ctx', [(i, i + 1) for i in range(...]
  transfers between devices with their start and end apart: 4 -> 0, of which waited for: 1 -> 0; matrix products, arithmetic and copies ran while one was open for 1% -> 0% of each run, Pallas kernels for 11% -> 0%
where the time goes in v2:
time: 318 us; the launch traced here: 317 us
  Pallas kernels  297 us (93%)
  other arithmetic  11.6 us (4%)
  between operations  5.13 us (2%)
  local copies, waits for them, and re-layouts  3.26 us (1%)
    pallas_call x1, Pallas kernels, line_local(): pl.pallas_call(functools.partial(line_kernel, dims), in_specs=[pl.BlockSp...  297 us
    div x1, other arithmetic, finish(): return ((product - alpha * vec) / beta, jnp.stack([alpha, beta]))  6.95 us

profile of v2, /device:TPU:0, one launch (start us, length us, event | category | flops | bytes accessed | tf_op | source)
XLA Modules:
  0.0 317.3 jit_solution(808612023550432491)
XLA Ops:
  0.7 0.1 broadcast_in_dim.102
  0.9 0.1 add.179
  1.0 0.8 copy.9
  1.9 0.1 fusion
  2.1 0.2 convert_reduce_fusion
  2.4 0.2 reduce_window_sum.22
  2.6 0.2 slice_reduce_fusion.1
  2.8 0.2 reduce_window_sum.27
  3.0 0.2 slice_reduce_fusion
  3.2 0.2 reduce_window_sum.23
  3.4 0.1 sub.84
  3.5 0.2 reduce_window_sum.32
  3.8 0.1 select_reduce_fusion.4
  3.9 0.1 select_reduce_fusion.3
  4.2 0.2 select_reduce_fusion
  4.4 0.8 fusion.3
  5.2 0.7 compare_select_fusion.3
  5.9 0.1 select_reduce_fusion.2
  6.1 0.6 concatenate.3.tab
  6.7 297.3 %shard_map.68 = (f32[1024,1024]{1,0:T(8,128)}, f32[3,8,128]{2,1,0:T(8,128)}) custom-call(s32[56]{0:T(128)} %concatenate.3.tab, bf16[1024,1024]{1,0:T(8,128)(2,1)} %q_ref.1, f32[1024,1024]{1,0:T(8,128)} %t_ref.1, bf16[2,8,128,1024]{3,2,1,0:T(8,128)(2,1)} %bitcast.29), custom_call_target="tpu_custom_call" | custom-call | tf_op jit(solution)/shard_map/pallas_call | solution.py:558
  303.9 0.8 reduce_sum.92
  304.7 0.6 fusion.17
  309.7 7.0 %subtract_divide_fusion = f32[1024,1024]{1,0:T(8,128)} fusion(f32[1024,1024]{1,0:T(8,128)} %get-tuple-element.4, f32[1024,1024]{1,0:T(8,128)} %t_ref.1, f32[]{:T(128)} %sqrt.3, f32[]{:T(128)} %div.133), kind=kLoop, calls=%fused_computation | loop fusion | flops 3145728 | bytes 12582920 | tf_op jit(solution)/shard_map/div | solution.py:225
  316.7 0.6 pad_maximum_fusion
  (23 shorter events, 0.9 us)

commit v3 on v2

--- a/solution.py
+++ b/solution.py
@@ -225,12 +225,13 @@
     return (product - alpha * vec) / beta, jnp.stack([alpha, beta])
 
 
-def line_kernel(dims, tab, q_ref, t_ref, kv_ref, out_ref, sum_ref, *scratch):
+def line_kernel(dims, tab, q_ref, t_ref, kv_ref, out_ref, coef_ref, *scratch):
     nb, heads, rand, nglob, cap, keep, nctx, nhead = dims
     rowbufs = scratch[:heads]
     ybufs = scratch[heads : 2 * heads]
-    (pool, ysend, left_order, glbuf, halo, red1, red2, right_s, right_r, left_s, left_r,
+    (pool_a, pool_b, sum_ref, ysend, left_order, glbuf, halo, red1, red2, right_s, right_r, left_s, left_r,
      y_s, y_r, gl_s, gl_r, halo_s, halo_r, red_s, red_r) = scratch[2 * heads :]
+    pools = (pool_a, pool_b)
     ny_slots = NZ * cap
     o_right, o_left = 0, nb
     o_y = 2 * nb
@@ -258,7 +259,7 @@
         place = pl.ds(pos_z * nb, count)
         target = me + NY if right else me - NY
         if s == 0 and not right:
-            source = left_order.at[c % 2, pl.ds(0, count)]
+            source = left_order.at[c % 3, pl.ds(0, count)]
         else:
             source = rowbufs[c].at[place]
         ss, rr = (right_s, right_r) if right else (left_s, left_r)
@@ -334,11 +335,11 @@
         each_hop(c, False, 0, lambda copy: copy.wait_send())
 
     def begin(c):
-        if c >= 2:
-            own_left_sent(c - 2)
+        if c >= 3:
+            own_left_sent(c - 3)
         for i in range(nb):
             rowbufs[c][z * nb + i] = kv_ref[:, tab[o_right + i], :, cols(c)]
-            left_order[c % 2, i] = kv_ref[:, tab[o_left + i], :, cols(c)]
+            left_order[c % 3, i] = kv_ref[:, tab[o_left + i], :, cols(c)]
         each_hop(c, True, 0, lambda copy: copy.start())
         each_hop(c, False, 0, lambda copy: copy.start())
 
@@ -365,26 +366,28 @@
             each_hop(c, True, s, lambda copy: copy.start())
             each_hop(c, False, s, lambda copy: copy.start())
 
-    def across(c):
+    def free_across(c):
         if c >= 2:
             y_copy(c - 2).wait_send()
             each_gl(c - 2, lambda copy: copy.wait_send())
+
+    def across(c, inner):
+        pool = pools[c % 2]
         pool[: NZ * nb] = rowbufs[c][...]
-
-        @pl.when((z == 0) | (z == last))
-        def _():
+        if not inner:
             gl_copy(c, True).wait_recv()
             pool[NZ * nb + ny_slots + nglob :] = glbuf[c]
-
         for g in range(nglob):
             ysend[c % 2, ny_slots + g] = pool[tab[o_g + g]]
-        each_gl(c, lambda copy: copy.start())
+        if inner:
+            each_gl(c, lambda copy: copy.start())
         for i in range(ny_slots):
             ysend[c % 2, i] = pool[tab[o_y + i]]
         y_copy(c).start()
 
     def compute(c):
         y_copy(c).wait_recv()
+        pool = pools[c % 2]
         pool[NZ * nb : NZ * nb + ny_slots + nglob] = ybufs[c][...]
 
         @pl.when(me > 0)
@@ -420,20 +423,36 @@
             sum_ref[2] += fold(t * t)
             return carry
 
-        lax.fori_loop(0, nb, body, 0)
+        lax.fori_loop(0, nb, body, 0, unroll=2)
 
     pl.semaphore_wait(barrier, nctx - 1 + nhead - 1)
     sum_ref[...] = jnp.zeros_like(sum_ref)
     begin(0)
+    if heads > 1:
+        begin(1)
+    relay(0, 1)
+    inner = (z > 0) & (z < last)
+    outer = (z == 0) | (z == last)
     for c in range(heads):
+        relay(c, 2)
+        free_across(c)
+
+        @pl.when(inner)
+        def _():
+            across(c, True)
+
         if c + 1 < heads:
-            begin(c + 1)
-        relay(c, 1)
+            relay(c + 1, 1)
+        if c + 2 < heads:
+            begin(c + 2)
         if c >= 1:
             compute(c - 1)
-        relay(c, 2)
         relay(c, 3)
-        across(c)
+
+        @pl.when(outer)
+        def _():
+            across(c, False)
+
     compute(heads - 1)
 
     def share(buf, axis, mine, count, base):
@@ -464,10 +483,29 @@
     share(red1, "head", hd, nhead, 0)
     share(red2, "ctx", me, nctx, nhead - 1)
 
+    def whole(i):
+        return jnp.sum(jnp.sum(sum_ref[i], axis=0, keepdims=True), axis=1, keepdims=True)
+
+    count = float(nb * BS * heads * HD * nctx * nhead)
+    cross, image_sum, vector = whole(0), whole(1), whole(2)
+    alpha = cross / count
+    square = image_sum - 2.0 * alpha * cross + alpha * alpha * vector
+    beta = jnp.sqrt(square / count + 1e-06)
+    coef_ref[0:1] = jnp.broadcast_to(alpha, (1, HD))
+    coef_ref[1:2] = jnp.broadcast_to(beta, (1, HD))
+    inverse_beta = 1.0 / beta
+
+    def scale(b, carry):
+        rows = pl.ds(pl.multiple_of(b * 16, 16), 16)
+        out_ref[rows, :] = (out_ref[rows, :] - alpha * t_ref[rows, :]) * inverse_beta
+        return carry
+
+    lax.fori_loop(0, nb * BS // 16, scale, 0)
+
     for c in range(heads):
         for s in range(last):
             each_hop(c, True, s, lambda copy: copy.wait_send())
-            if s > 0 or c >= heads - 2:
+            if s > 0 or c >= heads - 3:
                 each_hop(c, False, s, lambda copy: copy.wait_send())
 
         @pl.when(me < nctx - 1)
@@ -555,20 +593,22 @@
     unit = (2, BS, HD)
     vmem = pl.BlockSpec(memory_space=pltpu.VMEM)
     sem = pltpu.SemaphoreType.DMA
-    product, sums = pl.pallas_call(
+    next_vec, coefs = pl.pallas_call(
         functools.partial(line_kernel, dims),
         in_specs=[pl.BlockSpec(memory_space=pltpu.SMEM), vmem, vmem, vmem],
         out_specs=[vmem, vmem],
         out_shape=[
             jax.ShapeDtypeStruct((rows, cols), jnp.float32),
-            jax.ShapeDtypeStruct((3, 8, HD), jnp.float32),
+            jax.ShapeDtypeStruct((2, HD), jnp.float32),
         ],
         scratch_shapes=[pltpu.VMEM((NZ * nb,) + unit, jnp.bfloat16)] * heads
         + [pltpu.VMEM((slots,) + unit, jnp.bfloat16)] * heads
         + [
             pltpu.VMEM((NZ * nb + slots + nglob,) + unit, jnp.bfloat16),
+            pltpu.VMEM((NZ * nb + slots + nglob,) + unit, jnp.bfloat16),
+            pltpu.VMEM((3, 8, HD), jnp.float32),
             pltpu.VMEM((2, slots) + unit, jnp.bfloat16),
-            pltpu.VMEM((2, nb) + unit, jnp.bfloat16),
+            pltpu.VMEM((3, nb) + unit, jnp.bfloat16),
             pltpu.VMEM((heads, nglob) + unit, jnp.bfloat16),
             pltpu.VMEM((heads, 2) + unit, jnp.bfloat16),
             pltpu.VMEM((nhead, 3, 8, HD), jnp.float32),
@@ -582,7 +622,7 @@
             collective_id=0, has_side_effects=True, vmem_limit_bytes=VMEM_LIMIT
         ),
     )(tab, queries, lanczos_vec, key_value.reshape(2, nb, BS, cols))
-    return finish(product, lanczos_vec, jnp.sum(sums, axis=(1, 2)), float(rows * cols * n * nhead))
+    return next_vec, coefs[:, 0]
 
 
 def solution(mesh):

time: 318 us -> 314 us (0.987)
  other arithmetic: 11.6 us -> 3.27 us
  local copies, waits for them, and re-layouts: 3.26 us -> 8.71 us
  between operations: 5.13 us -> 0.75 us
  Pallas kernels: 297 us -> 301 us
    div x1 -> x0, other arithmetic: 6.95 us -> none  [finish(): return ((product - alpha * vec) / beta, jnp.stack([alpha, beta]))]
    unnamed x1 -> x2, local copies, waits for them, and re-layouts: 0.78 us -> 5.56 us
    pallas_call x1, Pallas kernels: 297 us -> 301 us  [line_local(): pl.pallas_call(functools.partial(line_kernel, dims), in_specs=[pl.BlockSp...]
where the time goes in v3:
time: 314 us
  Pallas kernels  301 us (96%)
  local copies, waits for them, and re-layouts  8.71 us (3%)
  other arithmetic  3.27 us (1%)
    pallas_call x1, Pallas kernels, line_local(): pl.pallas_call(functools.partial(line_kernel, dims), in_specs=[pl.BlockSp...  301 us

profile of v3, /device:TPU:0, one launch (start us, length us, event | category | flops | bytes accessed | tf_op | source)
XLA Modules:
  0.0 313.8 jit_solution(3322176580123710320)
XLA Ops:
  0.7 0.1 broadcast_in_dim.102
  0.9 0.1 add.173
  1.0 0.8 copy.9
  1.9 0.1 fusion
  2.1 0.2 convert_reduce_fusion
  2.4 0.2 reduce_window_sum.22
  2.6 0.2 slice_reduce_fusion.1
  2.8 0.2 reduce_window_sum.27
  3.0 0.2 slice_reduce_fusion
  3.2 0.2 reduce_window_sum.23
  3.4 0.1 sub.78
  3.5 0.2 reduce_window_sum.32
  3.8 0.1 select_reduce_fusion.4
  3.9 0.1 select_reduce_fusion.3
  4.0 0.1 sub.80
  4.1 0.1 sub.79
  4.2 0.2 select_reduce_fusion
  4.4 0.8 fusion.3
  5.2 0.7 compare_select_fusion.3
  5.9 0.1 select_reduce_fusion.2
  6.1 0.6 concatenate.3.tab
  6.7 301.0 %shard_map.68 = (f32[1024,1024]{1,0:T(8,128)}, f32[2,128]{1,0:T(2,128)}) custom-call(s32[56]{0:T(128)} %concatenate.3.tab, bf16[1024,1024]{1,0:T(8,128)(2,1)} %q_ref.1, f32[1024,1024]{1,0:T(8,128)} %t_ref.1, bf16[2,8,128,1024]{3,2,1,0:T(8,128)(2,1)} %bitcast.24), custom_call_target="tpu_custom_call" | custom-call | tf_op jit(solution)/shard_map/pallas_call | solution.py:596
  307.7 1.3 slice_reduce_fusion.2
  309.0 4.8 %copy.11 = f32[1024,1024]{1,0:T(8,128)} copy(f32[1024,1024]{1,0:T(8,128)} %get-tuple-element.32) | data formatting | bytes 8388608
  (21 shorter events, 0.8 us)

commit v4 on v3

--- a/solution.py
+++ b/solution.py
@@ -229,8 +229,9 @@
     nb, heads, rand, nglob, cap, keep, nctx, nhead = dims
     rowbufs = scratch[:heads]
     ybufs = scratch[heads : 2 * heads]
+    fars = scratch[2 * heads : 3 * heads]
     (pool_a, pool_b, sum_ref, ysend, left_order, glbuf, halo, red1, red2, right_s, right_r, left_s, left_r,
-     y_s, y_r, gl_s, gl_r, halo_s, halo_r, red_s, red_r) = scratch[2 * heads :]
+     y_s, y_r, yf_s, yf_r, yg_s, yg_r, gl_s, gl_r, halo_s, halo_r, red_s, red_r) = scratch[3 * heads :]
     pools = (pool_a, pool_b)
     ny_slots = NZ * cap
     o_right, o_left = 0, nb
@@ -264,16 +265,18 @@
             source = rowbufs[c].at[place]
         ss, rr = (right_s, right_r) if right else (left_s, left_r)
         return pltpu.make_async_remote_copy(
-            src_ref=source, dst_ref=rowbufs[c].at[place], send_sem=ss.at[c, s], recv_sem=rr.at[c, s],
+            src_ref=source, dst_ref=fars[c] if s == last - 1 else rowbufs[c].at[place], send_sem=ss.at[c, s], recv_sem=rr.at[c, s],
             device_id={"ctx": target}, device_id_type=MESH,
         )
 
     def each_hop(c, right, s, act):
         pos = z if right else last - z
 
-        @pl.when((pos >= s) & (pos < last - 1))
-        def _():
-            act(hop(c, right, s, nb))
+        if s < last - 1:
+
+            @pl.when((pos >= s) & (pos < last - 1))
+            def _():
+                act(hop(c, right, s, nb))
 
         @pl.when(pos == last - 1)
         def _():
@@ -286,15 +289,17 @@
         ss, rr = (right_s, right_r) if right else (left_s, left_r)
 
         def wait(count):
-            place = rowbufs[c].at[pl.ds(src_z * nb, count)]
+            place = fars[c] if s == last - 1 else rowbufs[c].at[pl.ds(src_z * nb, count)]
             pltpu.make_async_remote_copy(
                 src_ref=place, dst_ref=place, send_sem=ss.at[c, s], recv_sem=rr.at[c, s],
                 device_id={"ctx": peer}, device_id_type=MESH,
             ).wait_recv()
 
-        @pl.when((pos >= s + 1) & (pos < last))
-        def _():
-            wait(nb)
+        if s < last - 1:
+
+            @pl.when((pos >= s + 1) & (pos < last))
+            def _():
+                wait(nb)
 
         @pl.when(pos == last)
         def _():
@@ -366,27 +371,77 @@
             each_hop(c, True, s, lambda copy: copy.start())
             each_hop(c, False, s, lambda copy: copy.start())
 
+    far_z = jnp.where(z == 0, last, 0)
+    near_slot = jnp.where(z == 0, 0, cap)
+    inner = (z > 0) & (z < last)
+    outer = (z == 0) | (z == last)
+
+    def y_part(c, start, count, send, recv):
+        return pltpu.make_async_remote_copy(
+            src_ref=ysend.at[c % 2, pl.ds(start, count)], dst_ref=ybufs[c].at[pl.ds(start, count)],
+            send_sem=send.at[c], recv_sem=recv.at[c],
+            device_id={"ctx": peer}, device_id_type=MESH,
+        )
+
+    def y_near(c):
+        return y_part(c, near_slot, ny_slots - cap, y_s, y_r)
+
+    def y_far(c):
+        return y_part(c, far_z * cap, cap, yf_s, yf_r)
+
+    def y_glob(c):
+        return y_part(c, ny_slots, nglob, yg_s, yg_r)
+
+    def each_y(c, act):
+        @pl.when(inner)
+        def _():
+            act(y_copy(c))
+
+        @pl.when(outer)
+        def _():
+            act(y_near(c))
+            act(y_far(c))
+            act(y_glob(c))
+
     def free_across(c):
         if c >= 2:
-            y_copy(c - 2).wait_send()
+            each_y(c - 2, lambda copy: copy.wait_send())
             each_gl(c - 2, lambda copy: copy.wait_send())
 
-    def across(c, inner):
+    def across(c):
         pool = pools[c % 2]
         pool[: NZ * nb] = rowbufs[c][...]
-        if not inner:
+        for i in range(ny_slots):
+            ysend[c % 2, i] = pool[tab[o_y + i]]
+
+        @pl.when(inner)
+        def _():
+            for g in range(nglob):
+                ysend[c % 2, ny_slots + g] = pool[tab[o_g + g]]
+            each_gl(c, lambda copy: copy.start())
+            y_copy(c).start()
+
+        @pl.when(outer)
+        def _():
+            y_near(c).start()
+
+    def across_late(c):
+        pool = pools[c % 2]
+
+        @pl.when(outer)
+        def _():
+            pool[pl.ds(far_z * nb, keep)] = fars[c][...]
+            for k in range(cap):
+                ysend[c % 2, far_z * cap + k] = pool[tab[o_y + far_z * cap + k]]
+            y_far(c).start()
             gl_copy(c, True).wait_recv()
             pool[NZ * nb + ny_slots + nglob :] = glbuf[c]
-        for g in range(nglob):
-            ysend[c % 2, ny_slots + g] = pool[tab[o_g + g]]
-        if inner:
-            each_gl(c, lambda copy: copy.start())
-        for i in range(ny_slots):
-            ysend[c % 2, i] = pool[tab[o_y + i]]
-        y_copy(c).start()
+            for g in range(nglob):
+                ysend[c % 2, ny_slots + g] = pool[tab[o_g + g]]
+            y_glob(c).start()
 
     def compute(c):
-        y_copy(c).wait_recv()
+        each_y(c, lambda copy: copy.wait_recv())
         pool = pools[c % 2]
         pool[NZ * nb : NZ * nb + ny_slots + nglob] = ybufs[c][...]
 
@@ -423,7 +478,7 @@
             sum_ref[2] += fold(t * t)
             return carry
 
-        lax.fori_loop(0, nb, body, 0, unroll=2)
+        lax.fori_loop(0, nb, body, 0)
 
     pl.semaphore_wait(barrier, nctx - 1 + nhead - 1)
     sum_ref[...] = jnp.zeros_like(sum_ref)
@@ -431,16 +486,10 @@
     if heads > 1:
         begin(1)
     relay(0, 1)
-    inner = (z > 0) & (z < last)
-    outer = (z == 0) | (z == last)
     for c in range(heads):
         relay(c, 2)
         free_across(c)
-
-        @pl.when(inner)
-        def _():
-            across(c, True)
-
+        across(c)
         if c + 1 < heads:
             relay(c + 1, 1)
         if c + 2 < heads:
@@ -448,10 +497,7 @@
         if c >= 1:
             compute(c - 1)
         relay(c, 3)
-
-        @pl.when(outer)
-        def _():
-            across(c, False)
+        across_late(c)
 
     compute(heads - 1)
 
@@ -517,7 +563,7 @@
             halo_copy(c, False).wait_send()
 
         if c >= heads - 2:
-            y_copy(c).wait_send()
+            each_y(c, lambda copy: copy.wait_send())
             each_gl(c, lambda copy: copy.wait_send())
 
 
@@ -603,6 +649,7 @@
         ],
         scratch_shapes=[pltpu.VMEM((NZ * nb,) + unit, jnp.bfloat16)] * heads
         + [pltpu.VMEM((slots,) + unit, jnp.bfloat16)] * heads
+        + [pltpu.VMEM((keep,) + unit, jnp.bfloat16)] * heads
         + [
             pltpu.VMEM((NZ * nb + slots + nglob,) + unit, jnp.bfloat16),
             pltpu.VMEM((NZ * nb + slots + nglob,) + unit, jnp.bfloat16),
@@ -615,6 +662,7 @@
             pltpu.VMEM((n, 3, 8, HD), jnp.float32),
             sem((heads, NZ)), sem((heads, NZ)), sem((heads, NZ)), sem((heads, NZ)),
             sem((heads,)), sem((heads,)), sem((heads,)), sem((heads,)),
+            sem((heads,)), sem((heads,)), sem((heads,)), sem((heads,)),
             sem((heads, 2)), sem((heads, 2)),
             sem((n + nhead,)), sem((n + nhead,)),
         ],

time: 314 us -> 299 us (0.952)
  Pallas kernels: 301 us -> 287 us
    pallas_call x1, Pallas kernels: 301 us -> 287 us  [line_local(): pl.pallas_call(functools.partial(line_kernel, dims), in_specs=[pl.BlockSp...]
where the time goes in v4:
time: 299 us
  Pallas kernels  287 us (96%)
  local copies, waits for them, and re-layouts  8.71 us (3%)
  other arithmetic  3.27 us (1%)
    pallas_call x1, Pallas kernels, line_local(): pl.pallas_call(functools.partial(line_kernel, dims), in_specs=[pl.BlockSp...  287 us

profile of v4, /device:TPU:0, one launch (start us, length us, event | category | flops | bytes accessed | tf_op | source)
XLA Modules:
  0.0 299.3 jit_solution(3399793442817159750)
XLA Ops:
  0.7 0.1 broadcast_in_dim.102
  0.9 0.1 add.173
  1.0 0.8 copy.9
  1.9 0.1 fusion
  2.1 0.2 convert_reduce_fusion
  2.4 0.2 reduce_window_sum.22
  2.6 0.2 slice_reduce_fusion.1
  2.8 0.2 reduce_window_sum.27
  3.0 0.2 slice_reduce_fusion
  3.2 0.2 reduce_window_sum.23
  3.4 0.1 sub.78
  3.5 0.2 reduce_window_sum.32
  3.8 0.1 select_reduce_fusion.4
  3.9 0.1 select_reduce_fusion.3
  4.0 0.1 sub.80
  4.1 0.1 sub.79
  4.2 0.2 select_reduce_fusion
  4.4 0.8 fusion.3
  5.2 0.7 compare_select_fusion.3
  5.9 0.1 select_reduce_fusion.2
  6.1 0.6 concatenate.3.tab
  6.7 286.5 %shard_map.68 = (f32[1024,1024]{1,0:T(8,128)}, f32[2,128]{1,0:T(2,128)}) custom-call(s32[56]{0:T(128)} %concatenate.3.tab, bf16[1024,1024]{1,0:T(8,128)(2,1)} %q_ref.1, f32[1024,1024]{1,0:T(8,128)} %t_ref.1, bf16[2,8,128,1024]{3,2,1,0:T(8,128)(2,1)} %bitcast.24), custom_call_target="tpu_custom_call" | custom-call | tf_op jit(solution)/shard_map/pallas_call | solution.py:642
  293.2 1.3 slice_reduce_fusion.2
  294.5 4.8 %copy.11 = f32[1024,1024]{1,0:T(8,128)} copy(f32[1024,1024]{1,0:T(8,128)} %get-tuple-element.32) | data formatting | bytes 8388608
  (21 shorter events, 0.8 us)
